TPU v7x, 512 devices: a whole 4x4x16 slice. The times are simulated.
512 devices in a mesh: dp: 4 (over z_hi), cin: 32 (over y, x, core), cout: 4 (over z_lo).
Axes of the slice: x: 4, y: 4, z: 16 (z_hi: 4, z_lo: 4; z = z_hi * 4 + z_lo), core: 2. Of those that a mesh axis runs over, the one named last changes fastest.
Arguments:
- weight: bfloat16 [8, 2, 2048, 2048], P(None, None, 'cin', 'cout'), may hold values from -0.09375 to 0.09375
- spectrum: bfloat16 [8, 2, 2048, 2048], P(None, None, ('cin', 'cout'), 'dp'), may hold values from -0.1796875 to 0.1796875
- out_grad: bfloat16 [8, 2, 2048, 2048], P(None, None, ('cout', 'cin'), 'dp'), may hold values from -6 to 6
Outputs:
- spectrum_grad: bfloat16 [8, 2, 2048, 2048], P(None, None, ('cin', 'cout'), 'dp')
- weight_grad: bfloat16 [8, 2, 2048, 2048], P(None, None, 'cin', 'cout')
All inputs are finite; a program needn't handle non-finite values.
Results may differ from a plain program's by a relative error of at most 0.001.
Values may be sent and summed in bfloat16 or wider, within the bound.
No kernel may reach another device: no remote copies, remote signals or barrier semaphores. Data moves between devices by JAX's collectives and lax.ppermute only.
A program may use at most 64 MiB of HBM per device.

v0:
```python
import jax
import jax.numpy as jnp
from jax import lax
from jax.sharding import PartitionSpec as P


def block_terms(columns, rows_in, piece):
    w_real = columns[:, 0]
    w_imag = columns[:, 1]
    g_real = piece[:, 0]
    g_imag = piece[:, 1]
    x_real = rows_in[:, 0]
    x_imag = rows_in[:, 1]
    dx_real = jnp.einsum(
        "mio,mob->mib", w_real, g_real, preferred_element_type=jnp.float32
    ) + jnp.einsum("mio,mob->mib", w_imag, g_imag, preferred_element_type=jnp.float32)
    dx_imag = jnp.einsum(
        "mio,mob->mib", w_real, g_imag, preferred_element_type=jnp.float32
    ) - jnp.einsum("mio,mob->mib", w_imag, g_real, preferred_element_type=jnp.float32)
    dw_real = jnp.einsum(
        "mib,mob->mio", x_real, g_real, preferred_element_type=jnp.float32
    ) + jnp.einsum("mib,mob->mio", x_imag, g_imag, preferred_element_type=jnp.float32)
    dw_imag = jnp.einsum(
        "mib,mob->mio", x_real, g_imag, preferred_element_type=jnp.float32
    ) - jnp.einsum("mib,mob->mio", x_imag, g_real, preferred_element_type=jnp.float32)
    return (jnp.stack([dx_real, dx_imag], axis=1), jnp.stack([dw_real, dw_imag], axis=1))


def accumulate(weight, rows_in, grads):
    part_in, block = block_terms(weight, rows_in, lax.all_gather(grads, "cin", axis=2, tiled=True))
    return (part_in, block)


def on_device(weight, spectrum, out_grad):
    rows_in = lax.all_gather(spectrum, "cout", axis=2, tiled=True)
    term_in, term_weight = accumulate(weight, rows_in, out_grad)
    summed = lax.psum(term_weight, "dp")
    weight_grad = summed.astype(jnp.bfloat16)
    spectrum_grad = lax.psum_scatter(term_in, "cout", scatter_dimension=2, tiled=True).astype(
        jnp.bfloat16
    )
    return (spectrum_grad, weight_grad)


def solution(mesh):
    placed = (
        P(None, None, "cin", "cout"),
        P(None, None, ("cin", "cout"), "dp"),
        P(None, None, ("cout", "cin"), "dp"),
    )
    return jax.shard_map(
        on_device,
        mesh=mesh,
        in_specs=placed,
        out_specs=(P(None, None, ("cin", "cout"), "dp"), P(None, None, "cin", "cout")),
        check_vma=False,
    )
```

profile of v0, /device:TPU:34, one launch (start us, length us, event | category | flops | bytes accessed | tf_op | source)
XLA Modules:
  0.0 329.4 jit_solution(9001423755656557211)
XLA Ops:
  7.2 0.0 copy-start.1
  7.2 0.0 all-gather.3.cloned.1.call-start
  7.2 1.7 copy.6
  9.0 0.0 all-gather.3.cloned.1.call-update
  9.0 0.0 all-gather.5.cloned.1.call-start
  9.0 1.7 copy.8
  10.7 0.0 all-gather.5.cloned.1.call-update
  10.7 0.0 reduce-scatter.2.cloned.1.call-start
  10.8 73.4 %all-gather.3.cloned.1.call-done = bf16[8,2,512,512]{3,2,0,1:T(8,128)(2,1)} async-done(((bf16[8,2,16,512]{3,2,0,1:T(8,128)(2,1)}), bf16[8,2,512,512]{3,2,0,1:T(8,128)(2,1)}) %all-gather.3.cloned.1.call-update) | async-done | bytes 8388624 | tf_op jit(solution)/shard_map/all_gather | solution.py:30
  84.2 0.0 copy-start
  84.2 3.3 %fusion.3 = f32[8,64,512]{2,1,0:T(8,128)S(1)} fusion(bf16[8,2,512,512]{3,2,0,1:T(8,128)(2,1)} %all-gather.3.cloned.1.call-done, bf16[8,2,64,512]{3,2,1,0:T(8,128)(2,1)} %param.3), kind=kOutput, calls=%fused_computation.5 | convolution fusion | flops 268435456 | bytes 5767168 | tf_op jit(solution)/shard_map/mio,mob->mib/dot_general | solution.py:14
  87.5 0.0 copy-done.1
  87.5 3.5 %fusion.2 = f32[8,64,512]{2,1,0:T(8,128)S(1)} fusion(bf16[8,2,512,512]{3,2,0,1:T(8,128)(2,1)} %all-gather.3.cloned.1.call-done, bf16[8,2,64,512]{3,2,1,0:T(8,128)(2,1)S(1)} %copy-done.1), kind=kOutput, calls=%fused_computation.4 | convolution fusion | flops 268435456 | bytes 5767168 | tf_op jit(solution)/shard_map/mio,mob->mib/dot_general | solution.py:19
  91.0 0.0 copy-done
  91.0 0.8 fusion.9
  91.8 0.8 fusion.11
  92.6 1.5 pad_maximum_fusion
  94.1 0.0 reduce-scatter.2.cloned.1.call-update
  94.1 29.1 %all-gather.5.cloned.1.call-done = bf16[8,2,64,512]{3,2,0,1:T(8,128)(2,1)} async-done(((bf16[8,2,16,512]{3,2,0,1:T(8,128)(2,1)}), bf16[8,2,64,512]{3,2,0,1:T(8,128)(2,1)}) %all-gather.5.cloned.1.call-update) | async-done | bytes 1048592 | tf_op jit(solution)/shard_map/all_gather | solution.py:35
  123.2 0.0 copy-start.2
  123.2 0.0 slice-start
  123.2 3.9 %fusion.1 = f32[8,64,512]{2,1,0:T(8,128)S(1)} fusion(bf16[8,2,512,512]{3,2,0,1:T(8,128)(2,1)} %all-gather.3.cloned.1.call-done, bf16[8,2,64,512]{3,2,0,1:T(8,128)(2,1)} %all-gather.5.cloned.1.call-done), kind=kOutput, calls=%fused_computation.3 | convolution fusion | flops 268435456 | bytes 5767168 | tf_op jit(solution)/shard_map/mib,mob->mio/dot_general | solution.py:20
  127.1 0.0 copy-done.2
  127.1 0.0 slice-start.1
  127.1 3.7 %fusion = f32[8,64,512]{2,1,0:T(8,128)S(1)} fusion(bf16[8,2,512,512]{3,2,0,1:T(8,128)(2,1)} %all-gather.3.cloned.1.call-done, bf16[8,2,64,512]{3,2,0,1:T(8,128)(2,1)S(1)} %copy-done.2), kind=kOutput, calls=%fused_computation.2 | convolution fusion | flops 268435456 | bytes 5767168 | tf_op jit(solution)/shard_map/mib,mob->mio/dot_general | solution.py:25
  130.8 3.6 %fusion.13 = f32[8,1,64,512]{3,2,0,1:T(8,128)S(1)} fusion(f32[8,64,512]{2,1,0:T(8,128)S(1)} %fusion.1, bf16[8,2,512,512]{3,2,0,1:T(8,128)(2,1)} %all-gather.3.cloned.1.call-done, bf16[8,2,64,512]{3,2,0,1:T(8,128)(2,1)S(1)} %copy-done.2), kind=kOutput, calls=%fused_computation.17 | convolution fusion | flops 268697600 | bytes 6815744 | tf_op jit(solution)/shard_map/mib,mob->mio/dot_general | solution.py:22
  134.4 0.0 slice-done
  134.4 0.0 slice-done.1
  134.4 1.4 fusion.15
  135.8 0.2 pad_maximum_fusion.1
  136.0 184.0 %all-reduce.1 = bf16[8,2,64,512]{3,2,0,1:T(8,128)(2,1)S(1)} all-reduce(f32[8,2,64,512]{3,2,0,1:T(8,128)S(1)} %pad_maximum_fusion.1), channel_id=1, replica_groups=mesh['dp'=4,'cin'=32,'cout'=4] {'dp'}, use_global_device_ids=true, to_apply=%region_1.0 | all-reduce | flops 524288 | bytes 3145728 | tf_op jit(solution)/shard_map/psum | solution.py:37
  320.1 1.1 copy.10
  321.1 0.0 reduce-scatter.2.cloned.1.call-done
  321.1 1.1 convert_element_type.6
  322.2 0.7 copy.9
  (1 shorter events, 0.0 us)
Async XLA Ops:
  7.2 80.3 %copy-start.1 = (bf16[8,2,64,512]{3,2,1,0:T(8,128)(2,1)S(1)}, bf16[8,2,64,512]{3,2,1,0:T(8,128)(2,1)}, u32[]{:S(2)}) copy-start(bf16[8,2,64,512]{3,2,1,0:T(8,128)(2,1)} %param.3) | copy-start | bytes 3145732
  7.2 77.0 %all-gather.3.cloned.1.call-start = ((), (), s32[]{:S(2)}) async-start(), calls=%async_computation.1 | async-start | bytes 8650752 | tf_op jit(solution)/shard_map/all_gather | solution.py:30
  9.0 114.2 %all-gather.5.cloned.1.call-start = ((), (), s32[]{:S(2)}) async-start(), calls=%async_computation.3 | async-start | bytes 1310720 | tf_op jit(solution)/shard_map/all_gather | solution.py:35
  10.7 310.4 %reduce-scatter.2.cloned.1.call-start = ((), (), s32[]{:S(2)}) async-start(), calls=%async_computation.2 | async-start | bytes 2621440 | tf_op jit(solution)/shard_map/reduce_scatter | solution.py:39
  84.2 6.8 %copy-start = (bf16[8,2,512,512]{3,2,0,1:T(8,128)(2,1)S(1)}, bf16[8,2,512,512]{3,2,0,1:T(8,128)(2,1)}, u32[]{:S(2)}) copy-start(bf16[8,2,512,512]{3,2,0,1:T(8,128)(2,1)} %all-gather.3.cloned.1.call-done) | copy-start | bytes 25165828
  123.2 3.9 %copy-start.2 = (bf16[8,2,64,512]{3,2,0,1:T(8,128)(2,1)S(1)}, bf16[8,2,64,512]{3,2,0,1:T(8,128)(2,1)}, u32[]{:S(2)}) copy-start(bf16[8,2,64,512]{3,2,0,1:T(8,128)(2,1)} %all-gather.5.cloned.1.call-done) | copy-start | bytes 3145732
  123.2 11.2 %slice-start = ((s8[8388608]{0:T(1024)(128)(4,1)}), s8[4194304]{0:T(1024)(128)(4,1)S(1)}, s32[]{:S(2)}) async-start(s8[8388608]{0:T(1024)(128)(4,1)} %bitcast.58), calls=%async_computation.4 | async-start | bytes 8388608
  127.1 7.3 %slice-start.1 = ((s8[8388608]{0:T(1024)(128)(4,1)}), s8[4194304]{0:T(1024)(128)(4,1)S(1)}, s32[]{:S(2)}) async-start(s8[8388608]{0:T(1024)(128)(4,1)} %bitcast.58), calls=%async_computation.5 | async-start | bytes 8388608
Sparse Core Ops, SparseCore 0:
  11.8 72.3 all-gather.2
  86.8 36.3 all-gather.4
  126.0 147.0 reduce-scatter.1
where the time goes:
time: 330 us; the launch traced here: 329 us
  blocking collectives  184 us (56%)
  waiting for transfers between devices  102 us (31%)
  matrix products  20.9 us (6%)
  between operations  13.9 us (4%)
  local copies, waits for them, and re-layouts  5.23 us (2%)
    psum x1, blocking collectives, on_device(): summed = lax.psum(term_weight, 'dp')  184 us
    all_gather x1, waiting for transfers between devices, accumulate(): lax.all_gather(grads, 'cin', axis=2, tiled=True)  73.4 us
    all_gather x1, waiting for transfers between devices, on_device(): rows_in = lax.all_gather(spectrum, 'cout', axis=2, tiled=True)  29.1 us
  transfers between devices with their start and end apart: 3, of which 2 were waited for; matrix products, arithmetic and copies ran while one was open for 8% of the time, Pallas kernels for 0%

commit v1 on v0

--- a/solution.py
+++ b/solution.py
@@ -27,7 +27,13 @@
 
 
 def accumulate(weight, rows_in, grads):
-    part_in, block = block_terms(weight, rows_in, lax.all_gather(grads, "cin", axis=2, tiled=True))
+    part_in, block = block_terms(
+        weight,
+        rows_in,
+        jnp.concatenate(
+            lax.all_to_all(jnp.stack([grads] * lax.axis_size("cin")), "cin", 0, 0), axis=2
+        ),
+    )
     return (part_in, block)
 
 

time: 330 us -> 351 us (1.064)
  the two profiles are of different devices: /device:TPU:34 before, /device:TPU:64 now
where the time goes in v1:
time: 351 us
  blocking collectives  184 us (52%)
  waiting for transfers between devices  105 us (30%)
  matrix products  20.8 us (6%)
  local copies, waits for them, and re-layouts  15.9 us (5%)
  between operations  14.2 us (4%)
  starting transfers between devices  7.66 us (2%)
    psum x1, blocking collectives, on_device(): summed = lax.psum(term_weight, 'dp')  184 us
    all_to_all x1, waiting for transfers between devices, accumulate(): lax.all_to_all(jnp.stack([grads] * lax.axis_size('cin')), 'cin', 0, 0)  105 us
    reshape x1, local copies, waits for them, and re-layouts, accumulate(): jnp.concatenate(lax.all_to_all(jnp.stack([grads] * lax.axis_size('cin')),...  8.09 us
    all_to_all x1, starting transfers between devices, accumulate(): lax.all_to_all(jnp.stack([grads] * lax.axis_size('cin')), 'cin', 0, 0)  7.58 us
  transfers between devices with their start and end apart: 3, of which 1 were waited for; matrix products, arithmetic and copies ran while one was open for 9% of the time, Pallas kernels for 0%

profile of v1, /device:TPU:64, one launch (start us, length us, event | category | flops | bytes accessed | tf_op | source)
XLA Modules:
  0.0 350.7 jit_solution(12308804920906341240)
XLA Ops:
  7.2 1.0 copy.12
  8.1 4.3 %stack.14 = bf16[32,8,2,16,512]{4,3,1,2,0:T(8,128)(2,1)} broadcast(bf16[8,2,16,512]{3,2,0,1:T(8,128)(2,1)S(1)} %copy.12), dimensions={1,2,3,4} | broadcast | bytes 8650752 | tf_op jit(solution)/shard_map/stack | solution.py:34
  12.4 0.0 copy-start.3
  12.4 7.6 %all-to-all-start = ((bf16[32,8,2,16,512]{4,3,1,2,0:T(8,128)(2,1)}), bf16[32,8,2,16,512]{4,3,1,2,0:T(8,128)(2,1)}, u32[]{:S(2)}, u32[]{:S(2)}) async-start(bf16[32,8,2,16,512]{4,3,1,2,0:T(8,128)(2,1)} %stack.14), calls=%async_computation | async-start | bytes 16777216 | tf_op jit(solution)/shard_map/all_to_all | solution.py:34
  20.0 0.0 all-gather.2.cloned.1.call-start
  20.1 0.0 copy-done.3
  20.1 0.7 copy.15
  20.8 0.0 all-gather.2.cloned.1.call-update
  20.8 0.0 reduce-scatter.2.cloned.1.call-start
  20.9 105.0 %all-to-all-done = bf16[32,8,2,16,512]{4,3,1,2,0:T(8,128)(2,1)} async-done(((bf16[32,8,2,16,512]{4,3,1,2,0:T(8,128)(2,1)}), bf16[32,8,2,16,512]{4,3,1,2,0:T(8,128)(2,1)}, u32[]{:S(2)}, u32[]{:S(2)}) %all-to-all-start) | async-done | bytes 8388640 | tf_op jit(solution)/shard_map/all_to_all | solution.py:34
  125.9 0.0 copy-start.1
  125.9 8.1 %copy.13 = bf16[8,2,32,16,512]{4,3,2,0,1:T(8,128)(2,1)} copy(bf16[8,2,32,16,512]{4,3,0,1,2:T(8,128)(2,1)} %bitcast.1) | data formatting | bytes 16777216 | tf_op jit(solution)/shard_map/reshape | solution.py:33
  134.0 0.0 copy-done.1
  134.0 0.0 copy-start
  134.0 3.2 fusion.3
  137.2 3.5 fusion.2
  140.7 0.0 copy-done
  140.7 0.8 fusion.9
  141.5 0.8 fusion.11
  142.3 1.5 pad_maximum_fusion
  143.8 0.0 reduce-scatter.2.cloned.1.call-update
  143.8 0.0 all-gather.2.cloned.1.call-done
  143.9 0.0 copy-start.2
  143.9 0.0 slice-start
  143.9 3.9 %fusion.1 = f32[8,64,512]{2,1,0:T(8,128)S(1)} fusion(bf16[8,2,512,512]{3,2,0,1:T(8,128)(2,1)} %bitcast.62, bf16[8,2,64,512]{3,2,0,1:T(8,128)(2,1)} %all-gather.2.cloned.1.call-done), kind=kOutput, calls=%fused_computation.3 | convolution fusion | flops 268435456 | bytes 5767168 | tf_op jit(solution)/shard_map/mib,mob->mio/dot_general | solution.py:20
  147.7 0.0 copy-done.2
  147.8 0.0 slice-start.1
  147.8 3.7 %fusion = f32[8,64,512]{2,1,0:T(8,128)S(1)} fusion(bf16[8,2,512,512]{3,2,0,1:T(8,128)(2,1)} %bitcast.63, bf16[8,2,64,512]{3,2,0,1:T(8,128)(2,1)S(1)} %copy-done.2), kind=kOutput, calls=%fused_computation.2 | convolution fusion | flops 268435456 | bytes 5767168 | tf_op jit(solution)/shard_map/mib,mob->mio/dot_general | solution.py:25
  151.5 3.6 %fusion.13 = f32[8,1,64,512]{3,2,0,1:T(8,128)S(1)} fusion(f32[8,64,512]{2,1,0:T(8,128)S(1)} %fusion.1, bf16[8,2,512,512]{3,2,0,1:T(8,128)(2,1)} %bitcast.64, bf16[8,2,64,512]{3,2,0,1:T(8,128)(2,1)S(1)} %copy-done.2), kind=kOutput, calls=%fused_computation.17 | convolution fusion | flops 268697600 | bytes 6815744 | tf_op jit(solution)/shard_map/mib,mob->mio/dot_general | solution.py:22
  155.0 0.0 slice-done
  155.1 0.0 slice-done.1
  155.1 1.4 fusion.15
  156.4 0.2 pad_maximum_fusion.1
  156.7 184.3 %all-reduce.1 = bf16[8,2,64,512]{3,2,0,1:T(8,128)(2,1)S(1)} all-reduce(f32[8,2,64,512]{3,2,0,1:T(8,128)S(1)} %pad_maximum_fusion.1), channel_id=1, replica_groups=mesh['dp'=4,'cin'=32,'cout'=4] {'dp'}, use_global_device_ids=true, to_apply=%region_1.0 | all-reduce | flops 524288 | bytes 3145728 | tf_op jit(solution)/shard_map/psum | solution.py:43
  341.0 1.1 copy.17
  342.1 0.0 reduce-scatter.2.cloned.1.call-done
  342.1 1.1 convert_element_type.6
  343.2 0.7 copy.16
  (1 shorter events, 0.0 us)
Async XLA Ops:
  12.4 7.6 %copy-start.3 = (bf16[8,2,16,512]{3,2,1,0:T(8,128)(2,1)S(1)}, bf16[8,2,16,512]{3,2,1,0:T(8,128)(2,1)}, u32[]{:S(2)}) copy-start(bf16[8,2,16,512]{3,2,1,0:T(8,128)(2,1)} %param.4) | copy-start | bytes 786436
  12.4 113.5 %all-to-all-start = ((bf16[32,8,2,16,512]{4,3,1,2,0:T(8,128)(2,1)}), bf16[32,8,2,16,512]{4,3,1,2,0:T(8,128)(2,1)}, u32[]{:S(2)}, u32[]{:S(2)}) async-start(bf16[32,8,2,16,512]{4,3,1,2,0:T(8,128)(2,1)} %stack.14), calls=%async_computation | async-start | bytes 16777216 | tf_op jit(solution)/shard_map/all_to_all | solution.py:34
  20.0 123.8 %all-gather.2.cloned.1.call-start = ((), (), s32[]{:S(2)}) async-start(), calls=%async_computation.3 | async-start | bytes 1310720 | tf_op jit(solution)/shard_map/all_gather | solution.py:41
  20.8 321.3 %reduce-scatter.2.cloned.1.call-start = ((), (), s32[]{:S(2)}) async-start(), calls=%async_computation.2 | async-start | bytes 2621440 | tf_op jit(solution)/shard_map/reduce_scatter | solution.py:45
  125.9 8.1 %copy-start.1 = (bf16[8,2,64,512]{3,2,1,0:T(8,128)(2,1)S(1)}, bf16[8,2,64,512]{3,2,1,0:T(8,128)(2,1)}, u32[]{:S(2)}) copy-start(bf16[8,2,64,512]{3,2,1,0:T(8,128)(2,1)} %param.3) | copy-start | bytes 3145732
  134.0 6.7 %copy-start = (bf16[8,2,32,16,512]{4,3,2,0,1:T(8,128)(2,1)S(1)}, bf16[8,2,32,16,512]{4,3,2,0,1:T(8,128)(2,1)}, u32[]{:S(2)}) copy-start(bf16[8,2,32,16,512]{4,3,2,0,1:T(8,128)(2,1)} %copy.13) | copy-start | bytes 25165828
  143.9 3.9 %copy-start.2 = (bf16[8,2,64,512]{3,2,0,1:T(8,128)(2,1)S(1)}, bf16[8,2,64,512]{3,2,0,1:T(8,128)(2,1)}, u32[]{:S(2)}) copy-start(bf16[8,2,64,512]{3,2,0,1:T(8,128)(2,1)} %all-gather.2.cloned.1.call-done) | copy-start | bytes 3145732
  143.9 11.2 %slice-start = ((s8[8388608]{0:T(1024)(128)(4,1)}), s8[4194304]{0:T(1024)(128)(4,1)S(1)}, s32[]{:S(2)}) async-start(s8[8388608]{0:T(1024)(128)(4,1)} %bitcast.67), calls=%async_computation.4 | async-start | bytes 8388608
  147.8 7.3 %slice-start.1 = ((s8[8388608]{0:T(1024)(128)(4,1)}), s8[4194304]{0:T(1024)(128)(4,1)S(1)}, s32[]{:S(2)}) async-start(s8[8388608]{0:T(1024)(128)(4,1)} %bitcast.67), calls=%async_computation.5 | async-start | bytes 8388608
Sparse Core Ops, SparseCore 0:
  23.5 40.8 all-gather.1
  143.9 142.0 reduce-scatter.1

commit v2 on v0

--- a/solution.py
+++ b/solution.py
@@ -34,7 +34,7 @@
 def on_device(weight, spectrum, out_grad):
     rows_in = lax.all_gather(spectrum, "cout", axis=2, tiled=True)
     term_in, term_weight = accumulate(weight, rows_in, out_grad)
-    summed = lax.psum(term_weight, "dp")
+    summed = jnp.sum(lax.all_gather(term_weight, "dp"), axis=0)
     weight_grad = summed.astype(jnp.bfloat16)
     spectrum_grad = lax.psum_scatter(term_in, "cout", scatter_dimension=2, tiled=True).astype(
         jnp.bfloat16

time: 330 us -> 496 us (1.50)
  the two profiles are of different devices: /device:TPU:34 before, /device:TPU:1 now
where the time goes in v2:
time: 496 us
  waiting for transfers between devices  447 us (90%)
  matrix products  20.9 us (4%)
  between operations  13.9 us (3%)
  other arithmetic  8.81 us (2%)
  local copies, waits for them, and re-layouts  5.23 us (1%)
    all_gather x1, waiting for transfers between devices, on_device(): summed = jnp.sum(lax.all_gather(term_weight, 'dp'), axis=0)  299 us
    all_gather x1, waiting for transfers between devices, accumulate(): lax.all_gather(grads, 'cin', axis=2, tiled=True)  75 us
    reduce_scatter x1, waiting for transfers between devices, on_device(): lax.psum_scatter(term_in, 'cout', scatter_dimension=2, tiled=True)  42 us
    all_gather x1, waiting for transfers between devices, on_device(): rows_in = lax.all_gather(spectrum, 'cout', axis=2, tiled=True)  30.4 us
  transfers between devices with their start and end apart: 4, of which 4 were waited for; matrix products, arithmetic and copies ran while one was open for 6% of the time, Pallas kernels for 0%

profile of v2, /device:TPU:1, one launch (start us, length us, event | category | flops | bytes accessed | tf_op | source)
XLA Modules:
  0.0 495.9 jit_solution(13762476108574822858)
XLA Ops:
  7.2 0.0 copy-start.1
  7.2 0.0 all-gather.5.cloned.1.call-start
  7.2 1.7 copy.11
  9.0 0.0 all-gather.5.cloned.1.call-update
  9.0 0.0 all-gather.7.cloned.1.call-start
  9.0 1.7 copy.13
  10.7 0.0 all-gather.7.cloned.1.call-update
  10.7 0.0 reduce-scatter.2.cloned.1.call-start
  10.8 75.0 %all-gather.5.cloned.1.call-done = bf16[8,2,512,512]{3,2,0,1:T(8,128)(2,1)} async-done(((bf16[8,2,16,512]{3,2,0,1:T(8,128)(2,1)}), bf16[8,2,512,512]{3,2,0,1:T(8,128)(2,1)}) %all-gather.5.cloned.1.call-update) | async-done | bytes 8388624 | tf_op jit(solution)/shard_map/all_gather | solution.py:30
  85.8 0.0 copy-start
  85.8 3.3 fusion.2
  89.1 0.0 copy-done.1
  89.1 3.5 fusion.3
  92.6 0.0 copy-done
  92.6 0.8 fusion.11
  93.4 0.8 fusion.9
  94.2 1.5 pad_maximum_fusion
  95.8 0.0 reduce-scatter.2.cloned.1.call-update
  95.8 0.0 all-gather.9.cloned.1.call-start
  95.8 30.4 %all-gather.7.cloned.1.call-done = bf16[8,2,64,512]{3,2,0,1:T(8,128)(2,1)} async-done(((bf16[8,2,16,512]{3,2,0,1:T(8,128)(2,1)}), bf16[8,2,64,512]{3,2,0,1:T(8,128)(2,1)}) %all-gather.7.cloned.1.call-update) | async-done | bytes 1048592 | tf_op jit(solution)/shard_map/all_gather | solution.py:35
  126.2 0.0 copy-start.2
  126.2 0.0 slice-start
  126.2 3.9 fusion
  130.1 0.0 copy-done.2
  130.1 0.0 slice-start.1
  130.1 3.7 fusion.1
  133.8 3.6 fusion.15
  137.4 0.0 slice-done
  137.4 0.0 slice-done.1
  137.4 1.4 fusion.13
  138.8 1.6 pad_maximum_fusion.1
  140.4 0.0 all-gather.9.cloned.1.call-update
  140.4 42.0 %reduce-scatter.2.cloned.1.call-done = f32[8,2,16,512]{3,2,0,1:T(8,128)} async-done(((f32[8,2,64,512]{3,2,0,1:T(8,128)}), f32[8,2,16,512]{3,2,0,1:T(8,128)}) %reduce-scatter.2.cloned.1.call-update) | async-done | bytes 524304 | tf_op jit(solution)/shard_map/reduce_scatter | solution.py:39
  182.5 1.1 convert_element_type.6
  183.5 0.7 copy.14
  184.3 299.5 %all-gather.9.cloned.1.call-done = f32[32,2,64,512]{3,2,0,1:T(8,128)} async-done(((f32[8,2,64,512]{3,2,0,1:T(8,128)}), f32[32,2,64,512]{3,2,0,1:T(8,128)}) %all-gather.9.cloned.1.call-update) | async-done | bytes 8388624 | tf_op jit(solution)/shard_map/all_gather | solution.py:37
  483.7 4.6 reduce_sum.9
  488.3 1.1 copy.15
  (1 shorter events, 0.0 us)
Async XLA Ops:
  7.2 82.0 %copy-start.1 = (bf16[8,2,64,512]{3,2,1,0:T(8,128)(2,1)S(1)}, bf16[8,2,64,512]{3,2,1,0:T(8,128)(2,1)}, u32[]{:S(2)}) copy-start(bf16[8,2,64,512]{3,2,1,0:T(8,128)(2,1)} %param.3) | copy-start | bytes 3145732
  7.2 78.6 %all-gather.5.cloned.1.call-start = ((), (), s32[]{:S(2)}) async-start(), calls=%async_computation.1 | async-start | bytes 8650752 | tf_op jit(solution)/shard_map/all_gather | solution.py:30
  9.0 117.2 %all-gather.7.cloned.1.call-start = ((), (), s32[]{:S(2)}) async-start(), calls=%async_computation.3 | async-start | bytes 1310720 | tf_op jit(solution)/shard_map/all_gather | solution.py:35
  10.7 171.7 %reduce-scatter.2.cloned.1.call-start = ((), (), s32[]{:S(2)}) async-start(), calls=%async_computation.2 | async-start | bytes 2621440 | tf_op jit(solution)/shard_map/reduce_scatter | solution.py:39
  85.8 6.8 %copy-start = (bf16[8,2,512,512]{3,2,0,1:T(8,128)(2,1)S(1)}, bf16[8,2,512,512]{3,2,0,1:T(8,128)(2,1)}, u32[]{:S(2)}) copy-start(bf16[8,2,512,512]{3,2,0,1:T(8,128)(2,1)} %all-gather.5.cloned.1.call-done) | copy-start | bytes 25165828
  95.8 387.9 %all-gather.9.cloned.1.call-start = ((), (), s32[]{:S(2)}) async-start(), calls=%async_computation.4 | async-start | bytes 10485760 | tf_op jit(solution)/shard_map/all_gather | solution.py:37
  126.2 3.9 copy-start.2
  126.2 11.2 %slice-start = ((s8[8388608]{0:T(1024)(128)(4,1)}), s8[4194304]{0:T(1024)(128)(4,1)S(1)}, s32[]{:S(2)}) async-start(s8[8388608]{0:T(1024)(128)(4,1)} %bitcast.59), calls=%async_computation.5 | async-start | bytes 8388608
  130.1 7.3 %slice-start.1 = ((s8[8388608]{0:T(1024)(128)(4,1)}), s8[4194304]{0:T(1024)(128)(4,1)S(1)}, s32[]{:S(2)}) async-start(s8[8388608]{0:T(1024)(128)(4,1)} %bitcast.59), calls=%async_computation.6 | async-start | bytes 8388608
Sparse Core Ops, SparseCore 0:
  11.8 73.9 all-gather.4
  88.5 37.6 all-gather.6
  129.1 53.3 reduce-scatter.1
  184.6 299.0 all-gather.8
